TPU v7x, 32 devices: a whole 2x2x4 slice. The times are simulated.
32 devices in a mesh: tm: 8 (over z, y), space: 4 (over x, core).
Axes of the slice: x: 2, y: 2, z: 4, core: 2. Of those that a mesh axis runs over, the one named last changes fastest.
Arguments:
- prior_adjoint_iterate: float32 [8, 64, 128, 128], P('tm', 'space'), may hold values from -6 to 6
- material: int32 [64, 128, 128], P('space'), may hold values from 0 to 7
- probe_cell_index: int32 [256], P('space'), may hold values from 0 to 1048575, as said below
- misfit: float32 [8, 256], P('tm', 'space'), may hold values from -12 to 12
- ventilation_heat_loss: float32 [8], P('tm'), as said below
- conductance: float32 [8], replicated, may hold values from 0.03 to 0.14
- rock_heat_drain: float32 [8], replicated, as said below
Outputs:
- adjoint_new: float32 [8, 64, 128, 128], P('tm', 'space')
Inputs may be any that keep to these rules, and one draw needn't show every extreme that they name: `probe_cell_index`: sensors 64 p to 64 (p + 1) - 1 lie in the p-th block of 16 planes of the first dimension; a cell may hold several sensors. `ventilation_heat_loss`: Non-negative. `rock_heat_drain`: Positive.
All inputs are finite; a program needn't handle non-finite values.
Results may differ from a plain program's by a relative error of at most 0.00002.
Values sent between devices are 32-bit elements; how exact they have to be, the bound alone decides.
A program may use at most 64 MiB of HBM per device.

v0:
```python
import jax
import jax.numpy as jnp
from jax import lax
from jax.sharding import PartitionSpec as P

FINE_STEPS = 4


def padded_2(value, sides, width):
    for axis, dim in sides:
        size, length = (lax.axis_size(axis), value.shape[dim])
        up = [(i, (i + 1) % size) for i in range(size - 1)]
        down = [(j, i) for i, j in up]
        last = lax.slice_in_dim(value, length - width, length, axis=dim)
        initial = lax.slice_in_dim(value, 0, width, axis=dim)
        before = lax.ppermute(last, axis, up)
        after = lax.ppermute(initial, axis, down)
        value = jnp.concatenate([before, value, after], axis=dim)
    return value


def shifted(value, axis, steps):
    count = lax.axis_size(axis)
    initial, last = (max(0, -steps), min(count, count - steps))
    return lax.ppermute(value, axis, [(source, source + steps) for source in range(initial, last)])


def coarsen(field):
    split = field.reshape(field.shape[0] // 2, 2, field.shape[1] // 2, 2, field.shape[2])
    return 0.25 * (split[:, 0, :, 0] + split[:, 1, :, 0] + (split[:, 0, :, 1] + split[:, 1, :, 1]))


def refine(coarse):
    return jnp.repeat(jnp.repeat(coarse, 2, axis=0), 2, axis=1)


def neighbours(padded):
    x_sides = padded[2:, 1:-1, 1:-1] + padded[:-2, 1:-1, 1:-1]
    y_sides = padded[1:-1, 2:, 1:-1] + padded[1:-1, :-2, 1:-1]
    z_sides = padded[1:-1, 1:-1, 2:] + padded[1:-1, 1:-1, :-2]
    return x_sides + y_sides + z_sides


def lookup(material, values):
    summed = jnp.zeros(material.shape, jnp.float32)
    for rock_type in range(values.shape[0]):
        summed = summed + jnp.where(material == rock_type, values[rock_type], 0.0)
    return summed


def on_device(
    prior_adjoint_iterate,
    material,
    probe_cell_index,
    misfit,
    ventilation_heat_loss,
    conductance,
    rock_heat_drain,
):
    adjoint = prior_adjoint_iterate[0]
    planes = adjoint.shape[0]
    across = adjoint.shape[1]
    depth = adjoint.shape[2]
    cond_cell = lookup(material, conductance)
    cell_heat_drain = lookup(material, rock_heat_drain)
    drain_amounts = cell_heat_drain + ventilation_heat_loss[0]
    local_cell = probe_cell_index - lax.axis_index("space") * (planes * across * depth)
    source = (
        jnp.zeros((planes * across * depth,), jnp.float32)
        .at[local_cell]
        .add(misfit[0])
        .reshape(planes, across, depth)
    )
    seeded = adjoint + source
    current = seeded
    for sweep_index in range(FINE_STEPS):
        weighted = cond_cell * current
        padded_x = padded_2(weighted, (("space", 0),), 1)
        padded = jnp.pad(padded_x, ((0, 0), (1, 1), (1, 1)))
        current = current + (neighbours(padded) - 6.0 * weighted) - drain_amounts * current
    coarse_baseline = coarsen(cell_heat_drain)
    coarse_decay_rate = jnp.exp(-FINE_STEPS * (coarse_baseline + ventilation_heat_loss[0]))
    coarse_old = coarsen(adjoint)
    correction = current - refine(coarse_decay_rate * coarse_old)
    reduced = coarsen(correction)
    is_last = lax.axis_index("tm") == lax.axis_size("tm") - 1

    def advance(turn_index, chained):
        outgoing = coarse_decay_rate * chained + reduced
        arrived = shifted(outgoing, "tm", -1)
        return jnp.where(is_last, coarse_old, arrived)

    chained = lax.fori_loop(0, lax.axis_size("tm") - 1, advance, coarse_old)
    adjoint_new = refine(coarse_decay_rate * chained) + correction
    return adjoint_new[None]


def solution(mesh):
    in_specs = (
        P("tm", "space", None, None),
        P("space", None, None),
        P("space"),
        P("tm", "space"),
        P("tm"),
        P(),
        P(),
    )
    out_specs = P("tm", "space", None, None)
    return jax.shard_map(
        on_device, mesh=mesh, in_specs=in_specs, out_specs=out_specs, check_vma=False
    )
```

profile of v0, /device:TPU:0, one launch (start us, length us, event | category | flops | bytes accessed | tf_op | source)
XLA Modules:
  0.0 129.8 jit_solution(7823621715819305063)
XLA Ops:
  0.0 1.6 %fusion.51 = (f32[1]{0:T(128)}, f32[1]{0:T(128)}, f32[1]{0:T(128)}, f32[1]{0:T(128)}, f32[1]{0:T(128)}, /*index=5*/f32[1]{0:T(128)}, f32[1]{0:T(128)}, f32[1]{0:T(128)}) fusion(f32[8]{0:T(128)} %param.14), kind=kLoop, calls=%fused_computation.94 | loop fusion | bytes 64 | tf_op jit(solution)/shard_map/slice | solution.py:47
  2.3 1.3 %scatter_custom_fusion = f32[262144]{0:T(1024)S(1)} fusion(s32[64]{0:T(128)S(1)} %compare_select_fusion, f32[64]{0:T(128)} %bitcast.92, f32[]{:T(128)} %constant.21.clone.1), kind=kCustom, calls=%fused_computation.63 | custom fusion | flops 64 | bytes 1049088 | tf_op jit(solution)/shard_map/scatter-add | solution.py:71
  3.6 8.3 %fusion.30 = (f32[16,128,128]{2,1,0:T(8,128)S(1)}, f32[16,128,128]{2,1,0:T(8,128)S(1)}, pred[16,128,128]{2,1,0:T(8,128)(4,1)S(1)}, pred[16,128,128]{2,1,0:T(8,12...) fusion(f32[16,128,128]{2,1,0:T(8,128)S(1)} %bitcast.74, ...), kind=kLoop, calls=%fused_computation.73 | loop fusion | flops 6553600 | bytes 7340064 | tf_op jit(solution)/shard_map/mul | solution.py:77
  12.0 1.4 %collective-permute-start.1 = (f32[1,128,128]{2,1,0:T(8,128)S(1)}, f32[1,128,128]{2,1,0:T(8,128)S(1)}, u32[]{:S(2)}, u32[]{:S(2)}) collective-permute-start(f32[1,128,128]{2,1,0:T(8,128)S(1)} %get-tuple-element.85), channel_id=1, source_target_pairs={{1,0},{2,1},{3,2},{5,4},{6,5},{7,6},{9,8},{10,9},{11,10},{13,12},{... | collective-permute-start | bytes 196616 | tf_op jit(solution)/shard_map/ppermute | solution.py:17
  13.4 3.0 %collective-permute-start.2 = (f32[1,128,128]{2,1,0:T(8,128)S(1)}, f32[1,128,128]{2,1,0:T(8,128)S(1)}, u32[]{:S(2)}, u32[]{:S(2)}) collective-permute-start(f32[1,128,128]{2,1,0:T(8,128)S(1)} %get-tuple-element.84), channel_id=1, source_target_pairs={{0,1},{1,2},{2,3},{4,5},{5,6},{6,7},{8,9},{9,10},{10,11},{12,13},{... | collective-permute-start | bytes 196616 | tf_op jit(solution)/shard_map/ppermute | solution.py:16
  18.6 7.9 %fusion.39 = (f32[16,128,128]{2,1,0:T(8,128)S(1)}, f32[16,128,128]{2,1,0:T(8,128)}, f32[16,128,128]{2,1,0:T(8,128)S(1)}) fusion(f32[16,128,128]{2,1,0:T(8,128)S(1)} %get-tuple-element.58, f32[]{:T(128)} %bitcast.67, f32[16,128,128]{2,1,0:T(8,128)S(1)} %get-tuple-element.57, f32[18,130,130]{2,1,0:T(8,128)S(1)} %select_maximum_fusion.6, ...), kind=kLoop, calls=%fused_computation.84 | loop fusion | flops 7864320 | bytes 13762596 | tf_op jit(solution)/shard_map/mul | solution.py:77
  28.4 5.1 %collective-permute-start.4 = (f32[1,128,128]{2,1,0:T(8,128)}, f32[1,128,128]{2,1,0:T(8,128)S(1)}, u32[]{:S(2)}, u32[]{:S(2)}) collective-permute-start(f32[1,128,128]{2,1,0:T(8,128)} %get-tuple-element.78), channel_id=1, source_target_pairs={{0,1},{1,2},{2,3},{4,5},{5,6},{6,7},{8,9},{9,10},{10,11},{12,13},{... | collective-permute-start | bytes 196616 | tf_op jit(solution)/shard_map/ppermute | solution.py:16
  33.5 1.8 %fusion.49 = (f32[8,1,64,1,128]{4,3,2,1,0:T(1,128)S(1)}, f32[8,1,64,1,128]{4,3,2,1,0:T(1,128)}, f32[8,1,64,1,128]{4,3,2,1,0:T(1,128)}, f32[8,1,64,1,128]{4,3,2,1,0:T(1,128)}) fusion(f32[8,2,64,2,128]{4,3,2,1,0:T(2,128)S(1)} %bitcast.72), kind=kLoop, calls=%fused_computation.92 | loop fusion | bytes 2097152 | tf_op jit(solution)/shard_map/slice | solution.py:30
  37.8 1.3 collective-permute-start.5
  39.1 4.8 %collective-permute-start.6 = (f32[1,128,128]{2,1,0:T(8,128)S(1)}, f32[1,128,128]{2,1,0:T(8,128)S(1)}, u32[]{:S(2)}, u32[]{:S(2)}) collective-permute-start(f32[1,128,128]{2,1,0:T(8,128)S(1)} %get-tuple-element.76), channel_id=1, source_target_pairs={{0,1},{1,2},{2,3},{4,5},{5,6},{6,7},{8,9},{9,10},{10,11},{12,13},{... | collective-permute-start | bytes 196616 | tf_op jit(solution)/shard_map/ppermute | solution.py:16
  46.9 1.3 collective-permute-start.7
  48.2 4.9 %collective-permute-start.8 = (f32[1,128,128]{2,1,0:T(8,128)S(1)}, f32[1,128,128]{2,1,0:T(8,128)S(1)}, u32[]{:S(2)}, u32[]{:S(2)}) collective-permute-start(f32[1,128,128]{2,1,0:T(8,128)S(1)} %get-tuple-element.74), channel_id=1, source_target_pairs={{0,1},{1,2},{2,3},{4,5},{5,6},{6,7},{8,9},{9,10},{10,11},{12,13},{... | collective-permute-start | bytes 196616 | tf_op jit(solution)/shard_map/ppermute | solution.py:16
  57.1 71.1 %while.10 = (s32[]{:T(128)}, f32[8,64,128]{2,1,0:T(8,128)S(1)}, pred[]{:T(512)}, f32[8,64,128]{2,1,0:T(8,128)S(1)}, f32[8,64,128]{2,1,0:T(8,128)S(1)}, /*index=5*/f32[8,64,128]{2,1,0:T(8,128)S(1)}, s32[]{:T(128)}) while((s32[]{:T(128)}, f32[8,64,128]{2,1,0:T(8,128)S(1)}, pred[]{:T(512)}, f32[8,64,128]{2,1,0:T(8,128)S(1)}, ...), condition=%wide.region_2.3_spmd, body=%wide.region_1.2_spmd.sunk | while | flops 196610 | bytes 2883702 | solution.py:93
  57.1 1.3 collective-permute-start
  58.4 7.9 %collective-permute-done = f32[8,64,128]{2,1,0:T(8,128)S(1)} collective-permute-done((f32[8,64,128]{2,1,0:T(8,128)S(1)}, f32[8,64,128]{2,1,0:T(8,128)S(1)}, u32[]{:S(2)}, u32[]{:S(2)}) %collective-permute-start) | collective-permute-done | bytes 262176 | tf_op jit(solution)/shard_map/while/body/eval_jaxpr/ppermute | solution.py:25
  66.4 1.3 collective-permute-start
  67.7 9.2 %collective-permute-done = f32[8,64,128]{2,1,0:T(8,128)S(1)} collective-permute-done((f32[8,64,128]{2,1,0:T(8,128)S(1)}, f32[8,64,128]{2,1,0:T(8,128)S(1)}, u32[]{:S(2)}, u32[]{:S(2)}) %collective-permute-start) | collective-permute-done | bytes 262176 | tf_op jit(solution)/shard_map/while/body/eval_jaxpr/ppermute | solution.py:25
  77.0 1.3 collective-permute-start
  78.3 10.8 %collective-permute-done = f32[8,64,128]{2,1,0:T(8,128)S(1)} collective-permute-done((f32[8,64,128]{2,1,0:T(8,128)S(1)}, f32[8,64,128]{2,1,0:T(8,128)S(1)}, u32[]{:S(2)}, u32[]{:S(2)}) %collective-permute-start) | collective-permute-done | bytes 262176 | tf_op jit(solution)/shard_map/while/body/eval_jaxpr/ppermute | solution.py:25
  90.5 9.5 %collective-permute-done = f32[8,64,128]{2,1,0:T(8,128)S(1)} collective-permute-done((f32[8,64,128]{2,1,0:T(8,128)S(1)}, f32[8,64,128]{2,1,0:T(8,128)S(1)}, u32[]{:S(2)}, u32[]{:S(2)}) %collective-permute-start) | collective-permute-done | bytes 262176 | tf_op jit(solution)/shard_map/while/body/eval_jaxpr/ppermute | solution.py:25
  100.1 1.3 collective-permute-start
  101.4 8.6 %collective-permute-done = f32[8,64,128]{2,1,0:T(8,128)S(1)} collective-permute-done((f32[8,64,128]{2,1,0:T(8,128)S(1)}, f32[8,64,128]{2,1,0:T(8,128)S(1)}, u32[]{:S(2)}, u32[]{:S(2)}) %collective-permute-start) | collective-permute-done | bytes 262176 | tf_op jit(solution)/shard_map/while/body/eval_jaxpr/ppermute | solution.py:25
  111.3 7.6 %collective-permute-done = f32[8,64,128]{2,1,0:T(8,128)S(1)} collective-permute-done((f32[8,64,128]{2,1,0:T(8,128)S(1)}, f32[8,64,128]{2,1,0:T(8,128)S(1)}, u32[]{:S(2)}, u32[]{:S(2)}) %collective-permute-start) | collective-permute-done | bytes 262176 | tf_op jit(solution)/shard_map/while/body/eval_jaxpr/ppermute | solution.py:25
  120.4 7.8 %collective-permute-done = f32[8,64,128]{2,1,0:T(8,128)S(1)} collective-permute-done((f32[8,64,128]{2,1,0:T(8,128)S(1)}, f32[8,64,128]{2,1,0:T(8,128)S(1)}, u32[]{:S(2)}, u32[]{:S(2)}) %collective-permute-start) | collective-permute-done | bytes 262176 | tf_op jit(solution)/shard_map/while/body/eval_jaxpr/ppermute | solution.py:25
  (66 shorter events, 19.2 us)
Async XLA Ops:
  3.6 8.3 %copy-start.1 = (f32[262144]{0:T(1024)}, f32[262144]{0:T(1024)S(1)}, u32[]{:S(2)}) copy-start(f32[262144]{0:T(1024)S(1)} %scatter_custom_fusion) | copy-start | bytes 3145732
  3.6 13.5 %copy-start.7 = (f32[8]{0:T(128)S(1)}, f32[8]{0:T(128)}, u32[]{:S(2)}) copy-start(f32[8]{0:T(128)} %param.15) | copy-start | bytes 100
  11.9 6.6 %copy-start = (f32[1,16,128,128]{3,2,1,0:T(8,128)S(1)}, f32[1,16,128,128]{3,2,1,0:T(8,128)}, u32[]{:S(2)}) copy-start(f32[1,16,128,128]{3,2,1,0:T(8,128)} %param.9) | copy-start | bytes 3145732
  12.0 6.6 %copy-start.2 = (f32[262144]{0:T(1024)S(1)}, f32[262144]{0:T(1024)}, u32[]{:S(2)}) copy-start(f32[262144]{0:T(1024)} %copy-done.1) | copy-start | bytes 3145732
  12.0 5.8 %collective-permute-start.1 = (f32[1,128,128]{2,1,0:T(8,128)S(1)}, f32[1,128,128]{2,1,0:T(8,128)S(1)}, u32[]{:S(2)}, u32[]{:S(2)}) collective-permute-start(f32[1,128,128]{2,1,0:T(8,128)S(1)} %get-tuple-element.85), channel_id=1, source_target_pairs={{1,0},{2,1},{3,2},{5,4},{6,5},{7,6},{9,8},{10,9},{11,10},{13,12},{... | collective-permute-start | bytes 196616 | tf_op jit(solution)/shard_map/ppermute | solution.py:17
  13.4 4.4 %collective-permute-start.2 = (f32[1,128,128]{2,1,0:T(8,128)S(1)}, f32[1,128,128]{2,1,0:T(8,128)S(1)}, u32[]{:S(2)}, u32[]{:S(2)}) collective-permute-start(f32[1,128,128]{2,1,0:T(8,128)S(1)} %get-tuple-element.84), channel_id=1, source_target_pairs={{0,1},{1,2},{2,3},{4,5},{5,6},{6,7},{8,9},{9,10},{10,11},{12,13},{... | collective-permute-start | bytes 196616 | tf_op jit(solution)/shard_map/ppermute | solution.py:16
  27.2 8.2 %collective-permute-start.3 = (f32[1,128,128]{2,1,0:T(8,128)}, f32[1,128,128]{2,1,0:T(8,128)S(1)}, u32[]{:S(2)}, u32[]{:S(2)}) collective-permute-start(f32[1,128,128]{2,1,0:T(8,128)} %get-tuple-element.79), channel_id=1, source_target_pairs={{1,0},{2,1},{3,2},{5,4},{6,5},{7,6},{9,8},{10,9},{11,10},{13,12},{... | collective-permute-start | bytes 196616 | tf_op jit(solution)/shard_map/ppermute | solution.py:17
  28.4 6.9 %collective-permute-start.4 = (f32[1,128,128]{2,1,0:T(8,128)}, f32[1,128,128]{2,1,0:T(8,128)S(1)}, u32[]{:S(2)}, u32[]{:S(2)}) collective-permute-start(f32[1,128,128]{2,1,0:T(8,128)} %get-tuple-element.78), channel_id=1, source_target_pairs={{0,1},{1,2},{2,3},{4,5},{5,6},{6,7},{8,9},{9,10},{10,11},{12,13},{... | collective-permute-start | bytes 196616 | tf_op jit(solution)/shard_map/ppermute | solution.py:16
  35.3 1.2 copy-start.3
  37.8 7.0 %collective-permute-start.5 = (f32[1,128,128]{2,1,0:T(8,128)S(1)}, f32[1,128,128]{2,1,0:T(8,128)S(1)}, u32[]{:S(2)}, u32[]{:S(2)}) collective-permute-start(f32[1,128,128]{2,1,0:T(8,128)S(1)} %get-tuple-element.77), channel_id=1, source_target_pairs={{1,0},{2,1},{3,2},{5,4},{6,5},{7,6},{9,8},{10,9},{11,10},{13,12},{... | collective-permute-start | bytes 196616 | tf_op jit(solution)/shard_map/ppermute | solution.py:17
  39.1 5.8 %collective-permute-start.6 = (f32[1,128,128]{2,1,0:T(8,128)S(1)}, f32[1,128,128]{2,1,0:T(8,128)S(1)}, u32[]{:S(2)}, u32[]{:S(2)}) collective-permute-start(f32[1,128,128]{2,1,0:T(8,128)S(1)} %get-tuple-element.76), channel_id=1, source_target_pairs={{0,1},{1,2},{2,3},{4,5},{5,6},{6,7},{8,9},{9,10},{10,11},{12,13},{... | collective-permute-start | bytes 196616 | tf_op jit(solution)/shard_map/ppermute | solution.py:16
  45.6 7.5 %copy-start.4 = (f32[8,1,64,1,128]{4,3,2,1,0:T(1,128)S(1)}, f32[8,1,64,1,128]{4,3,2,1,0:T(1,128)}, u32[]{:S(2)}) copy-start(f32[8,1,64,1,128]{4,3,2,1,0:T(1,128)} %get-tuple-element.87) | copy-start | bytes 786436
  45.6 7.5 %copy-start.5 = (f32[8,1,64,1,128]{4,3,2,1,0:T(1,128)S(1)}, f32[8,1,64,1,128]{4,3,2,1,0:T(1,128)}, u32[]{:S(2)}) copy-start(f32[8,1,64,1,128]{4,3,2,1,0:T(1,128)} %get-tuple-element.88) | copy-start | bytes 786436
  45.6 7.5 %copy-start.6 = (f32[8,1,64,1,128]{4,3,2,1,0:T(1,128)S(1)}, f32[8,1,64,1,128]{4,3,2,1,0:T(1,128)}, u32[]{:S(2)}) copy-start(f32[8,1,64,1,128]{4,3,2,1,0:T(1,128)} %get-tuple-element.89) | copy-start | bytes 786436
  46.9 6.4 %collective-permute-start.7 = (f32[1,128,128]{2,1,0:T(8,128)S(1)}, f32[1,128,128]{2,1,0:T(8,128)S(1)}, u32[]{:S(2)}, u32[]{:S(2)}) collective-permute-start(f32[1,128,128]{2,1,0:T(8,128)S(1)} %get-tuple-element.75), channel_id=1, source_target_pairs={{1,0},{2,1},{3,2},{5,4},{6,5},{7,6},{9,8},{10,9},{11,10},{13,12},{... | collective-permute-start | bytes 196616 | tf_op jit(solution)/shard_map/ppermute | solution.py:17
  48.2 5.6 %collective-permute-start.8 = (f32[1,128,128]{2,1,0:T(8,128)S(1)}, f32[1,128,128]{2,1,0:T(8,128)S(1)}, u32[]{:S(2)}, u32[]{:S(2)}) collective-permute-start(f32[1,128,128]{2,1,0:T(8,128)S(1)} %get-tuple-element.74), channel_id=1, source_target_pairs={{0,1},{1,2},{2,3},{4,5},{5,6},{6,7},{8,9},{9,10},{10,11},{12,13},{... | collective-permute-start | bytes 196616 | tf_op jit(solution)/shard_map/ppermute | solution.py:16
  57.1 9.2 %collective-permute-start = (f32[8,64,128]{2,1,0:T(8,128)S(1)}, f32[8,64,128]{2,1,0:T(8,128)S(1)}, u32[]{:S(2)}, u32[]{:S(2)}) collective-permute-start(f32[8,64,128]{2,1,0:T(8,128)S(1)} %multiply_add_fusion.2), channel_id=1, source_target_pairs={{4,0},{8,4},{12,8},{16,12},{20,16},{24,20},{28,24},{5,1},{9,5},{13... | collective-permute-start | bytes 786440 | tf_op jit(solution)/shard_map/while/body/eval_jaxpr/ppermute | solution.py:25
  66.4 10.5 %collective-permute-start = (f32[8,64,128]{2,1,0:T(8,128)S(1)}, f32[8,64,128]{2,1,0:T(8,128)S(1)}, u32[]{:S(2)}, u32[]{:S(2)}) collective-permute-start(f32[8,64,128]{2,1,0:T(8,128)S(1)} %multiply_add_fusion.2), channel_id=1, source_target_pairs={{4,0},{8,4},{12,8},{16,12},{20,16},{24,20},{28,24},{5,1},{9,5},{13... | collective-permute-start | bytes 786440 | tf_op jit(solution)/shard_map/while/body/eval_jaxpr/ppermute | solution.py:25
  77.0 12.1 %collective-permute-start = (f32[8,64,128]{2,1,0:T(8,128)S(1)}, f32[8,64,128]{2,1,0:T(8,128)S(1)}, u32[]{:S(2)}, u32[]{:S(2)}) collective-permute-start(f32[8,64,128]{2,1,0:T(8,128)S(1)} %multiply_add_fusion.2), channel_id=1, source_target_pairs={{4,0},{8,4},{12,8},{16,12},{20,16},{24,20},{28,24},{5,1},{9,5},{13... | collective-permute-start | bytes 786440 | tf_op jit(solution)/shard_map/while/body/eval_jaxpr/ppermute | solution.py:25
  89.2 10.8 %collective-permute-start = (f32[8,64,128]{2,1,0:T(8,128)S(1)}, f32[8,64,128]{2,1,0:T(8,128)S(1)}, u32[]{:S(2)}, u32[]{:S(2)}) collective-permute-start(f32[8,64,128]{2,1,0:T(8,128)S(1)} %multiply_add_fusion.2), channel_id=1, source_target_pairs={{4,0},{8,4},{12,8},{16,12},{20,16},{24,20},{28,24},{5,1},{9,5},{13... | collective-permute-start | bytes 786440 | tf_op jit(solution)/shard_map/while/body/eval_jaxpr/ppermute | solution.py:25
  100.1 9.9 %collective-permute-start = (f32[8,64,128]{2,1,0:T(8,128)S(1)}, f32[8,64,128]{2,1,0:T(8,128)S(1)}, u32[]{:S(2)}, u32[]{:S(2)}) collective-permute-start(f32[8,64,128]{2,1,0:T(8,128)S(1)} %multiply_add_fusion.2), channel_id=1, source_target_pairs={{4,0},{8,4},{12,8},{16,12},{20,16},{24,20},{28,24},{5,1},{9,5},{13... | collective-permute-start | bytes 786440 | tf_op jit(solution)/shard_map/while/body/eval_jaxpr/ppermute | solution.py:25
  110.0 8.9 %collective-permute-start = (f32[8,64,128]{2,1,0:T(8,128)S(1)}, f32[8,64,128]{2,1,0:T(8,128)S(1)}, u32[]{:S(2)}, u32[]{:S(2)}) collective-permute-start(f32[8,64,128]{2,1,0:T(8,128)S(1)} %multiply_add_fusion.2), channel_id=1, source_target_pairs={{4,0},{8,4},{12,8},{16,12},{20,16},{24,20},{28,24},{5,1},{9,5},{13... | collective-permute-start | bytes 786440 | tf_op jit(solution)/shard_map/while/body/eval_jaxpr/ppermute | solution.py:25
  119.1 9.1 %collective-permute-start = (f32[8,64,128]{2,1,0:T(8,128)S(1)}, f32[8,64,128]{2,1,0:T(8,128)S(1)}, u32[]{:S(2)}, u32[]{:S(2)}) collective-permute-start(f32[8,64,128]{2,1,0:T(8,128)S(1)} %multiply_add_fusion.2), channel_id=1, source_target_pairs={{4,0},{8,4},{12,8},{16,12},{20,16},{24,20},{28,24},{5,1},{9,5},{13... | collective-permute-start | bytes 786440 | tf_op jit(solution)/shard_map/while/body/eval_jaxpr/ppermute | solution.py:25
where the time goes:
time: 132 us; the launch traced here: 130 us
  waiting for transfers between devices  61.8 us (47%)
  starting transfers between devices  32.2 us (24%)
  other arithmetic  26.7 us (20%)
  local copies, waits for them, and re-layouts  7.91 us (6%)
    ppermute x7, waiting for transfers between devices, shifted(): lax.ppermute(value, axis, [(source, source + steps) for source in range(i...  61.3 us
    mul x4, other arithmetic, on_device(): weighted = cond_cell * current  18.7 us
    ppermute x4, starting transfers between devices, padded_2(): before = lax.ppermute(last, axis, up)  17.8 us
    ppermute x7, starting transfers between devices, shifted(): lax.ppermute(value, axis, [(source, source + steps) for source in range(i...  9.04 us
    ppermute x4, starting transfers between devices, padded_2(): after = lax.ppermute(initial, axis, down)  5.29 us
    slice x3, local copies, waits for them, and re-layouts, coarsen(): split[:, 1, :, 0]  3.55 us
    concatenate x4, other arithmetic, padded_2(): value = jnp.concatenate([before, value, after], axis=dim)  2.85 us
  transfers between devices with their start and end apart: 15, of which 8 were waited for; matrix products, arithmetic and copies ran while one was open for 3% of the time, Pallas kernels for 0%

commit v1 on v0

v1 whole, which is shorter than its diff:
```python
import functools

import jax
import jax.numpy as jnp
from jax import lax
from jax.experimental import pallas as pl
from jax.experimental.pallas import tpu as pltpu
from jax.sharding import PartitionSpec as P

FINE_STEPS = 4
PAD = 8
F32 = jnp.float32
BF16 = jnp.bfloat16


def lookup(rock, tables):
    bits = [(rock & (1 << b)) != 0 for b in range(3)]
    found = []
    for table in tables:
        level = table
        for bit in bits:
            level = [jnp.where(bit, level[2 * n + 1], level[2 * n]) for n in range(len(level) // 2)]
        found.append(level[0])
    return found


def kernel(
    slabs, tiles,
    prior, material, probe, misfit, vent, conductance, drain,
    out,
    w, cond, keep, loss, rate, old, red,
    seen, mate_vent, my_vent, mate_red, gain, base, high_red, high_rate,
    chain_in, chain_out, swap_out, swap_in,
    vent_sem, halo_send, halo_recv, red_send, red_recv, chain_send, chain_recv, swap_send, swap_recv,
):
    t, p = lax.axis_index("tm"), lax.axis_index("space")
    planes, across, depth = prior.shape[1:]
    coarse = planes // 2
    half = coarse // 2
    rows = pl.ds(PAD, across)
    low = lax.rem(t, 2) == 0
    mate = jnp.where(low, t + 1, t - 1)
    has_lower, has_upper = t >= 2, t < slabs - 2
    has_left, has_right = p > 0, p < tiles - 1
    is_top = t == slabs - 1

    def own_plane(k):
        return jnp.where(low, half - 1 - k, half + k)

    def mate_plane(k):
        return jnp.where(low, half + k, half - 1 - k)

    barrier = pltpu.get_barrier_semaphore()

    def greet(axis, index):
        pl.semaphore_signal(barrier, inc=1, device_id={axis: index}, device_id_type=pl.DeviceIdType.MESH)

    greet("tm", mate)
    pl.when(has_lower)(lambda: greet("tm", t - 2))
    pl.when(has_upper)(lambda: greet("tm", t + 2))
    pl.when(has_left)(lambda: greet("space", p - 1))
    pl.when(has_right)(lambda: greet("space", p + 1))

    def send(src, dst, send_sem, recv_sem, axis, index):
        return pltpu.make_async_remote_copy(
            src_ref=src, dst_ref=dst, send_sem=send_sem, recv_sem=recv_sem,
            device_id={axis: index}, device_id_type=pl.DeviceIdType.MESH,
        )

    def vent_copy():
        return send(my_vent, mate_vent, vent_sem.at[0], vent_sem.at[1], "tm", mate)

    def left_copy(n):
        return send(w.at[n, 1, rows], w.at[n, planes + 1, rows], halo_send.at[n, 0], halo_recv.at[n, 0], "space", p - 1)

    def right_copy(n):
        return send(w.at[n, planes, rows], w.at[n, 0, rows], halo_send.at[n, 1], halo_recv.at[n, 1], "space", p + 1)

    def red_copy(k):
        return send(red.at[mate_plane(k)], mate_red.at[k], red_send.at[k], red_recv.at[k], "tm", mate)

    def chain_copy(k):
        return send(chain_out.at[k], chain_in.at[k], chain_send.at[k], chain_recv.at[k], "tm", t - 2)

    def swap_copy(k):
        return send(swap_out.at[k], swap_in.at[k], swap_send.at[k], swap_recv.at[k], "tm", mate)

    extra = vent[0]
    cond_of = [conductance[m] for m in range(conductance.shape[0])]
    drain_of = [drain[m] for m in range(drain.shape[0])]

    cell = probe[...] - p * (planes * across * depth)
    cell_row, cell_lane = cell // depth, lax.rem(cell, depth)
    amount = misfit[...]
    first = amount.astype(BF16)
    rest = amount - first.astype(F32)
    second = rest.astype(BF16)
    third = rest - second.astype(F32)
    place = lax.broadcasted_iota(jnp.int32, (depth, cell.shape[1]), 0) == cell_lane
    for n, term in enumerate((first.astype(F32), second.astype(F32), third)):
        seen[n] = jnp.where(place, term, 0.0).astype(BF16)

    def seed(i):
        number = lax.broadcasted_iota(jnp.int32, (across, cell.shape[1]), 0) + i * across
        hit = jnp.where(number == cell_row, 1.0, 0.0).astype(BF16)
        added = sum(
            lax.dot_general(hit, seen[n], (((1,), (1,)), ((), ())), preferred_element_type=F32)
            for n in range(3)
        )
        c, l = lookup(material[i], (cond_of, drain_of))
        cond[i] = c
        loss[i] = l
        keep[i] = 1.0 - 6.0 * c - (l + extra)
        w[0, i + 1, rows] = c * (prior[0, i] + added)

    edge = jnp.zeros((PAD, depth), F32)

    def clear(i, _):
        for n in range(FINE_STEPS):
            w[n, i + 1, pl.ds(0, PAD)] = edge
            w[n, i + 1, pl.ds(PAD + across, PAD)] = edge
        return 0

    lax.fori_loop(0, planes, clear, 0)
    seed(0)
    seed(planes - 1)
    my_vent[...] = jnp.full(my_vent.shape, extra, F32)

    @pl.when(jnp.logical_not(has_left))
    def _():
        for n in range(FINE_STEPS):
            w[n, 0, rows] = jnp.zeros((across, depth), F32)

    @pl.when(jnp.logical_not(has_right))
    def _():
        for n in range(FINE_STEPS):
            w[n, planes + 1, rows] = jnp.zeros((across, depth), F32)

    @pl.when(jnp.logical_not(has_upper))
    def _():
        chain_in[...] = jnp.zeros(chain_in.shape, F32)

    count = 1 + has_lower.astype(jnp.int32) + has_upper.astype(jnp.int32)
    count = count + has_left.astype(jnp.int32) + has_right.astype(jnp.int32)
    pl.semaphore_wait(barrier, count)

    def send_faces(n):
        pl.when(has_left)(lambda: left_copy(n).start())
        pl.when(has_right)(lambda: right_copy(n).start())

    def wait_faces(n):
        pl.when(has_right)(lambda: left_copy(n).wait_recv())
        pl.when(has_left)(lambda: right_copy(n).wait_recv())

    send_faces(0)
    vent_copy().start()

    lax.fori_loop(1, planes - 1, lambda i, c: (seed(i), c)[1], 0)

    def four(ref, q):
        even, odd = pl.ds(0, across // 2, stride=2), pl.ds(1, across // 2, stride=2)
        a, b = ref.at[2 * q], ref.at[2 * q + 1]
        return 0.25 * ((a[even, :] + b[even, :]) + (a[odd, :] + b[odd, :]))

    def prepare(q, _):
        rate[q] = jnp.exp(-FINE_STEPS * (four(loss, q) + extra))
        old[q] = four(prior.at[0], q)
        return 0

    lax.fori_loop(0, coarse, prepare, 0)

    lane = lax.broadcasted_iota(jnp.int32, (across, depth), 1)

    def around(n, i):
        here = w[n, i + 1, rows]
        x_sides = w[n, i, rows] + w[n, i + 2, rows]
        y_sides = w[n, i + 1, pl.ds(PAD - 1, across)] + w[n, i + 1, pl.ds(PAD + 1, across)]
        before = jnp.where(lane == 0, 0.0, pltpu.roll(here, 1, 1))
        after = jnp.where(lane == depth - 1, 0.0, pltpu.roll(here, depth - 1, 1))
        return here, x_sides + y_sides + (before + after)

    def step(n, i):
        here, sides = around(n, i)
        w[n + 1, i + 1, rows] = keep[i] * here + cond[i] * sides

    for n in range(FINE_STEPS - 1):
        wait_faces(n)
        step(n, 0)
        step(n, planes - 1)
        send_faces(n + 1)
        lax.fori_loop(1, planes - 1, lambda i, c: (step(n, i), c)[1], 0)

    def finish(i):
        here, sides = around(FINE_STEPS - 1, i)
        out[0, i] = keep[i] * here / cond[i] + sides

    def reduce(q):
        mean = four(out.at[0], q)
        red[q] = jnp.where(is_top, mean, mean - rate[q] * old[q])

    def last_step(k):
        for q in (half - 1 - k, half + k):
            finish(2 * q)
            finish(2 * q + 1)
            reduce(q)
        red_copy(k).start()

    lax.fori_loop(0, half - 1, lambda k, c: (last_step(k), c)[1], 0)
    wait_faces(FINE_STEPS - 1)
    last_step(half - 1)
    vent_copy().wait_recv()

    def combine(k, _):
        q = own_plane(k)
        mine = rate[q]
        his = jnp.exp(-FINE_STEPS * (four(loss, q) + mate_vent[0:1, :]))
        red_copy(k).wait_recv()
        low_rate, upper_rate = jnp.where(low, mine, his), jnp.where(low, his, mine)
        low_red, upper_red = jnp.where(low, red[q], mate_red[k]), jnp.where(low, mate_red[k], red[q])
        gain[k] = low_rate * upper_rate
        base[k] = low_red + low_rate * upper_red
        high_red[k] = upper_red
        high_rate[k] = upper_rate
        return 0

    lax.fori_loop(0, half, combine, 0)

    def add_carry(q, carry):
        moved = jnp.where(is_top, 0.0, rate[q] * (carry - old[q]))
        for i in (2 * q, 2 * q + 1):
            plane = out.at[0, i]
            for phase in range(2):
                pick = pl.ds(phase, across // 2, stride=2)
                plane[pick, :] = plane[pick, :] + moved

    def link(k, _):
        pl.when(has_upper)(lambda: chain_copy(k).wait_recv())
        entering = chain_in[k]
        chain_out[k] = base[k] + gain[k] * entering
        pl.when(has_lower)(lambda: chain_copy(k).start())
        lower = high_red[k] + high_rate[k] * entering
        swap_out[k] = jnp.where(low, entering, lower)
        swap_copy(k).start()
        add_carry(own_plane(k), jnp.where(low, lower, entering))
        return 0

    lax.fori_loop(0, half, link, 0)

    def close(k, _):
        swap_copy(k).wait_recv()
        add_carry(mate_plane(k), swap_in[k])
        return 0

    lax.fori_loop(0, half, close, 0)

    vent_copy().wait_send()
    for n in range(FINE_STEPS):
        pl.when(has_left)(lambda: left_copy(n).wait_send())
        pl.when(has_right)(lambda: right_copy(n).wait_send())
    for k in range(half):
        red_copy(k).wait_send()
        pl.when(has_lower)(lambda: chain_copy(k).wait_send())
        swap_copy(k).wait_send()


def on_device(slabs, tiles, prior, material, probe, misfit, vent, conductance, drain):
    planes, across, depth = prior.shape[1:]
    coarse, half = planes // 2, planes // 4
    sensors = probe.shape[0]
    vmem, smem = pl.BlockSpec(memory_space=pltpu.VMEM), pl.BlockSpec(memory_space=pltpu.SMEM)
    whole = pltpu.VMEM((planes, across, depth), F32)
    quarter = pltpu.VMEM((coarse, across // 2, depth), F32)
    eighth = pltpu.VMEM((half, across // 2, depth), F32)
    small = pltpu.VMEM((8, depth), F32)
    dma = pltpu.SemaphoreType.DMA
    return pl.pallas_call(
        functools.partial(kernel, slabs, tiles),
        out_shape=jax.ShapeDtypeStruct(prior.shape, F32),
        in_specs=[vmem, vmem, vmem, vmem, smem, smem, smem],
        out_specs=vmem,
        scratch_shapes=[
            pltpu.VMEM((FINE_STEPS, planes + 2, across + 2 * PAD, depth), F32),
            whole, whole, whole, quarter, quarter, quarter,
            pltpu.VMEM((3, depth, sensors), BF16),
            small, small, eighth, eighth, eighth, eighth, eighth,
            eighth, eighth, eighth, eighth,
            dma((2,)), dma((FINE_STEPS, 2)), dma((FINE_STEPS, 2)),
            dma((half,)), dma((half,)), dma((half,)), dma((half,)), dma((half,)), dma((half,)),
        ],
        compiler_params=pltpu.CompilerParams(
            collective_id=0, has_side_effects=True, vmem_limit_bytes=48 * 1024 * 1024
        ),
    )(prior, material, probe.reshape(1, sensors), misfit, vent, conductance, drain)


def solution(mesh):
    in_specs = (
        P("tm", "space", None, None),
        P("space", None, None),
        P("space"),
        P("tm", "space"),
        P("tm"),
        P(),
        P(),
    )
    out_specs = P("tm", "space", None, None)
    run = functools.partial(on_device, mesh.shape["tm"], mesh.shape["space"])
    return jax.shard_map(run, mesh=mesh, in_specs=in_specs, out_specs=out_specs, check_vma=False)
```

time: 132 us -> 38.5 us (0.29); the launches traced: 130 us -> 38.3 us
  waiting for transfers between devices: 61.8 us -> 0 us
  Pallas kernels: 0 us -> 33.5 us
  starting transfers between devices: 32.2 us -> 0 us
  other arithmetic: 26.7 us -> 0 us
  local copies, waits for them, and re-layouts: 7.91 us -> 4.08 us
    ppermute x15 -> x0, waiting for transfers between devices: 61.8 us -> none  [the longest x7 61.3 us: shifted(): lax.ppermute(value, axis, [(source, source + steps) for source in range(i...]
    pallas_call x0 -> x1, Pallas kernels: none -> 33.5 us  [on_device(): pl.pallas_call(functools.partial(kernel, slabs, tiles), out_shape=jax.Sha...]
    ppermute x15 -> x0, starting transfers between devices: 32.2 us -> none  [the longest x4 17.8 us: padded_2(): before = lax.ppermute(last, axis, up)]
    mul x7 -> x0, other arithmetic: 19 us -> none  [the longest x4 18.7 us: on_device(): weighted = cond_cell * current]
    slice x9 -> x0, local copies, waits for them, and re-layouts: 6.55 us -> none  [the longest x3 3.55 us: coarsen(): split[:, 1, :, 0]]
    unnamed x17 -> x13, local copies, waits for them, and re-layouts: 0.55 us -> 4.08 us
    concatenate x4 -> x0, other arithmetic: 2.85 us -> none  [padded_2(): value = jnp.concatenate([before, value, after], axis=dim)]
  transfers between devices with their start and end apart: 15 -> 0, of which waited for: 8 -> 0; matrix products, arithmetic and copies ran while one was open for 3% -> 0% of each run, Pallas kernels for 0% -> 0%
where the time goes in v1:
time: 38.5 us; the launch traced here: 38.3 us
  Pallas kernels  33.5 us (87%)
  local copies, waits for them, and re-layouts  4.08 us (11%)
  between operations  0.71 us (2%)
    pallas_call x1, Pallas kernels, on_device(): pl.pallas_call(functools.partial(kernel, slabs, tiles), out_shape=jax.Sha...  33.5 us
    unnamed x13, local copies, waits for them, and re-layouts  4.08 us

profile of v1, /device:TPU:0, one launch (start us, length us, event | category | flops | bytes accessed | tf_op | source)
XLA Modules:
  0.0 38.3 jit_solution(8992086135033358104)
XLA Ops:
  0.0 0.0 copy-start.5
  0.7 0.0 copy-start.2
  0.7 0.0 copy-start.3
  0.7 0.0 copy-start.4
  0.7 0.0 copy-done.5
  0.7 0.6 %copy-done.2 = s32[64]{0:T(128)S(1)} copy-done((s32[64]{0:T(128)S(1)}, s32[64]{0:T(128)}, u32[]{:S(2)}) %copy-start.2) | copy-done | bytes 280
  1.3 0.0 copy-done.3
  1.3 0.0 copy-done.4
  1.4 0.0 copy-start
  1.4 1.2 %copy-done = f32[1,16,128,128]{3,2,1,0:T(8,128)S(1)} copy-done((f32[1,16,128,128]{3,2,1,0:T(8,128)S(1)}, f32[1,16,128,128]{3,2,1,0:T(8,128)}, u32[]{:S(2)}) %copy-start) | copy-done | bytes 1048600
  2.6 0.0 copy-start.1
  2.6 1.2 %copy-done.1 = s32[16,128,128]{2,1,0:T(8,128)S(1)} copy-done((s32[16,128,128]{2,1,0:T(8,128)S(1)}, s32[16,128,128]{2,1,0:T(8,128)}, u32[]{:S(2)}) %copy-start.1) | copy-done | bytes 1048600
  3.8 33.5 %shard_map.73 = f32[1,16,128,128]{3,2,1,0:T(8,128)S(1)} custom-call(f32[1,16,128,128]{3,2,1,0:T(8,128)S(1)} %copy-done, s32[16,128,128]{2,1,0:T(8,128)S(1)} %copy-done.1, s32[1,64]{1,0:T(1,128)S(1)} %bitcast.1, f32[1,64]{1,0:T(1,128)S(1)} %copy-done.3, f32[1]{0:T(128)S(6)} %copy.9.vent, f32[8]{0:T(128)S(1)} %copy-done.4, f32[8]{0:T(128)S(1)} %copy-done.5), custom_call_target="tpu_custom_call" | custom-call | tf_op jit(solution)/shard_map/pallas_call | solution.py:276
  37.3 1.0 %copy.10 = f32[1,16,128,128]{3,2,1,0:T(8,128)} copy(f32[1,16,128,128]{3,2,1,0:T(8,128)S(1)} %shard_map.73) | data formatting | bytes 2097152
Async XLA Ops:
  0.0 0.7 %copy-start.5 = (f32[8]{0:T(128)S(1)}, f32[8]{0:T(128)}, u32[]{:S(2)}) copy-start(f32[8]{0:T(128)} %drain.1) | copy-start | bytes 100
  0.7 0.7 %copy-start.2 = (s32[64]{0:T(128)S(1)}, s32[64]{0:T(128)}, u32[]{:S(2)}) copy-start(s32[64]{0:T(128)} %param.9) | copy-start | bytes 772
  0.7 0.7 %copy-start.3 = (f32[1,64]{1,0:T(1,128)S(1)}, f32[1,64]{1,0:T(1,128)}, u32[]{:S(2)}) copy-start(f32[1,64]{1,0:T(1,128)} %misfit.1) | copy-start | bytes 772
  0.7 0.7 %copy-start.4 = (f32[8]{0:T(128)S(1)}, f32[8]{0:T(128)}, u32[]{:S(2)}) copy-start(f32[8]{0:T(128)} %conductance.1) | copy-start | bytes 100
  1.4 1.2 %copy-start = (f32[1,16,128,128]{3,2,1,0:T(8,128)S(1)}, f32[1,16,128,128]{3,2,1,0:T(8,128)}, u32[]{:S(2)}) copy-start(f32[1,16,128,128]{3,2,1,0:T(8,128)} %prior.1) | copy-start | bytes 3145732
  2.6 1.2 %copy-start.1 = (s32[16,128,128]{2,1,0:T(8,128)S(1)}, s32[16,128,128]{2,1,0:T(8,128)}, u32[]{:S(2)}) copy-start(s32[16,128,128]{2,1,0:T(8,128)} %material.1) | copy-start | bytes 3145732

commit v2 on v1

v2 whole, which is shorter than its diff:
```python
import functools

import jax
import jax.numpy as jnp
from jax import lax
from jax.experimental import pallas as pl
from jax.experimental.pallas import tpu as pltpu
from jax.sharding import PartitionSpec as P

FINE_STEPS = 4
PAD = 8
CUT = 2
UNROLL = 2
F32 = jnp.float32
BF16 = jnp.bfloat16


def lookup(rock, tables):
    bits = [(rock & (1 << b)) != 0 for b in range(3)]
    found = []
    for table in tables:
        level = table
        for bit in bits:
            level = [jnp.where(bit, level[2 * n + 1], level[2 * n]) for n in range(len(level) // 2)]
        found.append(level[0])
    return found


def kernel(
    slabs, tiles,
    prior_in, material_in, probe_in, misfit_in, vent_in, conductance_in, drain_in,
    out,
    prior, material, probe, misfit, vent, conductance, drain, in_sem,
    w, cond, keep, loss, rate, old, red,
    seen, mate_vent, my_vent, mate_red, gain, base, high_red, high_rate,
    chain_in, chain_out, swap_out, swap_in, carried,
    vent_sem, halo_send, halo_recv, red_send, red_recv, chain_send, chain_recv, swap_send, swap_recv,
):
    t, p = lax.axis_index("tm"), lax.axis_index("space")
    planes, across, depth = prior.shape[1:]
    coarse = planes // 2
    half = coarse // 2
    chunks = half * CUT
    part = across // 2 // CUT
    inner = pl.ds(1, planes - 2)
    small = [(probe_in, probe), (misfit_in, misfit), (vent_in, vent), (conductance_in, conductance), (drain_in, drain)]
    faces, body = [], []
    for i in (0, planes - 1):
        faces += [(prior_in.at[0, i], prior.at[0, i]), (material_in.at[i], material.at[i])]
    body += [(material_in.at[inner], material.at[inner]), (prior_in.at[0, inner], prior.at[0, inner])]
    loads = [pltpu.make_async_copy(a, b, in_sem.at[n]) for n, (a, b) in enumerate(small + faces + body)]
    for load in loads:
        load.start()
    rows = pl.ds(PAD, across)
    low = lax.rem(t, 2) == 0
    mate = jnp.where(low, t + 1, t - 1)
    has_lower, has_upper = t >= 2, t < slabs - 2
    has_left, has_right = p > 0, p < tiles - 1
    is_top = t == slabs - 1

    def own_chunk(c):
        k, r = c // CUT, c % CUT
        return jnp.where(low, half - 1 - k, half + k) * CUT + r

    def mate_chunk(c):
        k, r = c // CUT, c % CUT
        return jnp.where(low, half + k, half - 1 - k) * CUT + r

    barrier = pltpu.get_barrier_semaphore()

    def greet(axis, index):
        pl.semaphore_signal(barrier, inc=1, device_id={axis: index}, device_id_type=pl.DeviceIdType.MESH)

    greet("tm", mate)
    pl.when(has_lower)(lambda: greet("tm", t - 2))
    pl.when(has_upper)(lambda: greet("tm", t + 2))
    pl.when(has_left)(lambda: greet("space", p - 1))
    pl.when(has_right)(lambda: greet("space", p + 1))

    def send(src, dst, send_sem, recv_sem, axis, index):
        return pltpu.make_async_remote_copy(
            src_ref=src, dst_ref=dst, send_sem=send_sem, recv_sem=recv_sem,
            device_id={axis: index}, device_id_type=pl.DeviceIdType.MESH,
        )

    def vent_copy():
        return send(my_vent, mate_vent, vent_sem.at[0], vent_sem.at[1], "tm", mate)

    def left_copy(n):
        return send(w.at[n, 1, rows], w.at[n, planes + 1, rows], halo_send.at[n, 0], halo_recv.at[n, 0], "space", p - 1)

    def right_copy(n):
        return send(w.at[n, planes, rows], w.at[n, 0, rows], halo_send.at[n, 1], halo_recv.at[n, 1], "space", p + 1)

    def red_copy(k):
        return send(red.at[mate_chunk(k)], mate_red.at[k], red_send.at[k], red_recv.at[k], "tm", mate)

    def chain_copy(k):
        return send(chain_out.at[k], chain_in.at[k], chain_send.at[k], chain_recv.at[k], "tm", t - 2)

    def swap_copy(k):
        return send(swap_out.at[k], swap_in.at[k], swap_send.at[k], swap_recv.at[k], "tm", mate)

    edge = jnp.zeros((PAD, depth), F32)

    def clear(i, _):
        for n in range(FINE_STEPS):
            w[n, i + 1, pl.ds(0, PAD)] = edge
            w[n, i + 1, pl.ds(PAD + across, PAD)] = edge
        return 0

    lax.fori_loop(0, planes, clear, 0)

    @pl.when(jnp.logical_not(has_left))
    def _():
        for n in range(FINE_STEPS):
            w[n, 0, rows] = jnp.zeros((across, depth), F32)

    @pl.when(jnp.logical_not(has_right))
    def _():
        for n in range(FINE_STEPS):
            w[n, planes + 1, rows] = jnp.zeros((across, depth), F32)

    for load in loads[: len(small)]:
        load.wait()
    extra = vent[0]
    cond_of = [conductance[m] for m in range(conductance.shape[0])]
    drain_of = [drain[m] for m in range(drain.shape[0])]

    cell = probe[...] - p * (planes * across * depth)
    cell_row, cell_lane = cell // depth, lax.rem(cell, depth)
    amount = misfit[...]
    first = amount.astype(BF16)
    rest = amount - first.astype(F32)
    second = rest.astype(BF16)
    third = rest - second.astype(F32)
    place = lax.broadcasted_iota(jnp.int32, (depth, cell.shape[1]), 0) == cell_lane
    for n, term in enumerate((first.astype(F32), second.astype(F32), third)):
        seen[n] = jnp.where(place, term, 0.0).astype(BF16)

    def seed(i):
        number = lax.broadcasted_iota(jnp.int32, (across, cell.shape[1]), 0) + i * across
        hit = jnp.where(number == cell_row, 1.0, 0.0).astype(BF16)
        added = sum(
            lax.dot_general(hit, seen[n], (((1,), (1,)), ((), ())), preferred_element_type=F32)
            for n in range(3)
        )
        c, l = lookup(material[i], (cond_of, drain_of))
        cond[i] = c
        loss[i] = l
        keep[i] = 1.0 - 6.0 * c - (l + extra)
        w[0, i + 1, rows] = c * (prior[0, i] + added)

    for load in loads[len(small) : len(small) + len(faces)]:
        load.wait()
    seed(0)
    seed(planes - 1)
    my_vent[...] = jnp.full(my_vent.shape, extra, F32)
    count = 1 + has_lower.astype(jnp.int32) + has_upper.astype(jnp.int32)
    count = count + has_left.astype(jnp.int32) + has_right.astype(jnp.int32)
    pl.semaphore_wait(barrier, count)

    def send_faces(n):
        pl.when(has_left)(lambda: left_copy(n).start())
        pl.when(has_right)(lambda: right_copy(n).start())

    def wait_faces(n):
        pl.when(has_right)(lambda: left_copy(n).wait_recv())
        pl.when(has_left)(lambda: right_copy(n).wait_recv())

    send_faces(0)
    vent_copy().start()

    for load in loads[len(small) + len(faces) :]:
        load.wait()
    lax.fori_loop(1, planes - 1, lambda i, c: (seed(i), c)[1], 0, unroll=2)

    def four(ref, j):
        q, r = j // CUT, j % CUT
        start = 2 * part * r
        even, odd = pl.ds(start, part, stride=2), pl.ds(start + 1, part, stride=2)
        a, b = ref.at[2 * q], ref.at[2 * q + 1]
        return 0.25 * ((a[even, :] + b[even, :]) + (a[odd, :] + b[odd, :]))

    def prepare(j, _):
        rate[j] = jnp.exp(-FINE_STEPS * (four(loss, j) + extra))
        old[j] = four(prior.at[0], j)
        return 0

    lax.fori_loop(0, coarse * CUT, prepare, 0, unroll=2)

    lane = lax.broadcasted_iota(jnp.int32, (across, depth), 1)

    def around(n, i):
        here = w[n, i + 1, rows]
        x_sides = w[n, i, rows] + w[n, i + 2, rows]
        y_sides = w[n, i + 1, pl.ds(PAD - 1, across)] + w[n, i + 1, pl.ds(PAD + 1, across)]
        before = jnp.where(lane == 0, 0.0, pltpu.roll(here, 1, 1))
        after = jnp.where(lane == depth - 1, 0.0, pltpu.roll(here, depth - 1, 1))
        return here, x_sides + y_sides + (before + after)

    def step(n, i):
        here, sides = around(n, i)
        w[n + 1, i + 1, rows] = keep[i] * here + cond[i] * sides

    for n in range(FINE_STEPS - 1):
        wait_faces(n)
        step(n, 0)
        step(n, planes - 1)
        send_faces(n + 1)
        lax.fori_loop(1, planes - 1, lambda i, c: (step(n, i), c)[1], 0, unroll=UNROLL)

    def finish(i):
        here, sides = around(FINE_STEPS - 1, i)
        out[0, i] = keep[i] * here / cond[i] + sides

    def reduce(j):
        mean = four(out.at[0], j)
        red[j] = jnp.where(is_top, mean, mean - rate[j] * old[j])

    def last_step(k):
        for q in (half - 1 - k, half + k):
            finish(2 * q)
            finish(2 * q + 1)
            for r in range(CUT):
                reduce(q * CUT + r)
        for r in range(CUT):
            red_copy(k * CUT + r).start()

    lax.fori_loop(0, half - 1, lambda k, c: (last_step(k), c)[1], 0)
    wait_faces(FINE_STEPS - 1)
    last_step(half - 1)
    vent_copy().wait_recv()

    def combine(c, _):
        j = own_chunk(c)
        mine = rate[j]
        his = jnp.exp(-FINE_STEPS * (four(loss, j) + mate_vent[0:1, :]))
        red_copy(c).wait_recv()
        low_rate, upper_rate = jnp.where(low, mine, his), jnp.where(low, his, mine)
        low_red, upper_red = jnp.where(low, red[j], mate_red[c]), jnp.where(low, mate_red[c], red[j])
        gain[c] = low_rate * upper_rate
        base[c] = low_red + low_rate * upper_red
        high_red[c] = upper_red
        high_rate[c] = upper_rate

        @pl.when(jnp.logical_not(has_upper))
        def _():
            chain_out[c] = low_red + low_rate * upper_red
            pl.when(has_lower)(lambda: chain_copy(c).start())

        return 0

    lax.fori_loop(0, chunks, combine, 0)

    def add_carry(j, carry):
        q, r = j // CUT, j % CUT
        moved = jnp.where(is_top, 0.0, rate[j] * (carry - old[j]))
        for i in (2 * q, 2 * q + 1):
            plane = out.at[0, i]
            for phase in range(2):
                pick = pl.ds(2 * part * r + phase, part, stride=2)
                plane[pick, :] = plane[pick, :] + moved

    def pass_on(c, entering):
        lower = high_red[c] + high_rate[c] * entering
        swap_out[c] = jnp.where(low, entering, lower)
        swap_copy(c).start()
        carried[c] = jnp.where(low, lower, entering)

    @pl.when(has_upper)
    def _():
        def link(c, _):
            chain_copy(c).wait_recv()
            entering = chain_in[c]
            chain_out[c] = base[c] + gain[c] * entering
            pl.when(has_lower)(lambda: chain_copy(c).start())
            pass_on(c, entering)
            return 0

        lax.fori_loop(0, chunks, link, 0)

    @pl.when(jnp.logical_not(has_upper))
    def _():
        def link(c, _):
            pass_on(c, jnp.zeros((part, depth), F32))
            return 0

        lax.fori_loop(0, chunks, link, 0)

    def own(c, _):
        add_carry(own_chunk(c), carried[c])
        return 0

    lax.fori_loop(0, chunks, own, 0)

    def close(c, _):
        swap_copy(c).wait_recv()
        add_carry(mate_chunk(c), swap_in[c])
        return 0

    lax.fori_loop(0, chunks, close, 0)

    vent_copy().wait_send()
    for n in range(FINE_STEPS):
        pl.when(has_left)(lambda: left_copy(n).wait_send())
        pl.when(has_right)(lambda: right_copy(n).wait_send())
    for k in range(chunks):
        red_copy(k).wait_send()
        pl.when(has_lower)(lambda: chain_copy(k).wait_send())
        swap_copy(k).wait_send()


def on_device(slabs, tiles, prior, material, probe, misfit, vent, conductance, drain):
    planes, across, depth = prior.shape[1:]
    pieces, chunks, part = planes // 2 * CUT, planes // 4 * CUT, across // 2 // CUT
    sensors = probe.shape[0]
    vmem, hbm = pl.BlockSpec(memory_space=pltpu.VMEM), pl.BlockSpec(memory_space=pltpu.HBM)
    whole = pltpu.VMEM((planes, across, depth), F32)
    quarter = pltpu.VMEM((pieces, part, depth), F32)
    eighth = pltpu.VMEM((chunks, part, depth), F32)
    small = pltpu.VMEM((8, depth), F32)
    dma = pltpu.SemaphoreType.DMA
    return pl.pallas_call(
        functools.partial(kernel, slabs, tiles),
        out_shape=jax.ShapeDtypeStruct(prior.shape, F32),
        in_specs=[hbm] * 7,
        out_specs=vmem,
        scratch_shapes=[
            pltpu.VMEM(prior.shape, F32), pltpu.VMEM(material.shape, jnp.int32),
            pltpu.VMEM((1, sensors), jnp.int32), pltpu.VMEM(misfit.shape, F32),
            pltpu.SMEM(vent.shape, F32), pltpu.SMEM(conductance.shape, F32), pltpu.SMEM(drain.shape, F32),
            dma((11,)),
            pltpu.VMEM((FINE_STEPS, planes + 2, across + 2 * PAD, depth), F32),
            whole, whole, whole, quarter, quarter, quarter,
            pltpu.VMEM((3, depth, sensors), BF16),
            small, small, eighth, eighth, eighth, eighth, eighth,
            eighth, eighth, eighth, eighth, eighth,
            dma((2,)), dma((FINE_STEPS, 2)), dma((FINE_STEPS, 2)),
            dma((chunks,)), dma((chunks,)), dma((chunks,)), dma((chunks,)), dma((chunks,)), dma((chunks,)),
        ],
        compiler_params=pltpu.CompilerParams(
            collective_id=0, has_side_effects=True, vmem_limit_bytes=60 * 1024 * 1024
        ),
    )(prior, material, probe.reshape(1, sensors), misfit, vent, conductance, drain)


def solution(mesh):
    in_specs = (
        P("tm", "space", None, None),
        P("space", None, None),
        P("space"),
        P("tm", "space"),
        P("tm"),
        P(),
        P(),
    )
    out_specs = P("tm", "space", None, None)
    run = functools.partial(on_device, mesh.shape["tm"], mesh.shape["space"])
    return jax.shard_map(run, mesh=mesh, in_specs=in_specs, out_specs=out_specs, check_vma=False)
```

time: 38.5 us -> 34.4 us (0.89)
  Pallas kernels: 33.5 us -> 31.3 us
  local copies, waits for them, and re-layouts: 4.08 us -> 2.3 us
    pallas_call x1, Pallas kernels: 33.5 us -> 31.3 us  [on_device(): pl.pallas_call(functools.partial(kernel, slabs, tiles), out_shape=jax.Sha...]
    unnamed x13 -> x1, local copies, waits for them, and re-layouts: 4.08 us -> 2.3 us
where the time goes in v2:
time: 34.4 us; the launch traced here: 34.3 us
  Pallas kernels  31.3 us (91%)
  local copies, waits for them, and re-layouts  2.3 us (7%)
  between operations  0.66 us (2%)
    pallas_call x1, Pallas kernels, on_device(): pl.pallas_call(functools.partial(kernel, slabs, tiles), out_shape=jax.Sha...  31.3 us
    unnamed x1, local copies, waits for them, and re-layouts  2.3 us

profile of v2, /device:TPU:0, one launch (start us, length us, event | category | flops | bytes accessed | tf_op | source)
XLA Modules:
  0.0 34.3 jit_solution(11889542011422620677)
XLA Ops:
  0.7 31.3 %shard_map.73 = f32[1,16,128,128]{3,2,1,0:T(8,128)} custom-call(f32[1,16,128,128]{3,2,1,0:T(8,128)} %prior_in.1, s32[16,128,128]{2,1,0:T(8,128)} %material_in.1, s32[1,64]{1,0:T(1,128)} %bitcast.1, f32[1,64]{1,0:T(1,128)} %misfit_in.1, f32[1]{0:T(128)S(6)} %copy.9.vent_in, f32[8]{0:T(128)} %conductance_in.1, f32[8]{0:T(128)} %drain_in.1), custom_call_target="tpu_custom_call" | custom-call | tf_op jit(solution)/shard_map/pallas_call | solution.py:324
  32.0 2.3 %copy.10 = f32[1,16,128,128]{3,2,1,0:T(8,128)} copy(f32[1,16,128,128]{3,2,1,0:T(8,128)} %shard_map.73) | data formatting | bytes 2097152

commit v3 on v2

--- a/solution.py
+++ b/solution.py
@@ -28,9 +28,9 @@
 
 def kernel(
     slabs, tiles,
-    prior_in, material_in, probe_in, misfit_in, vent_in, conductance_in, drain_in,
+    prior_in, material_in, probe_in, misfit_in, conductance_in, drain_in, vent,
     out,
-    prior, material, probe, misfit, vent, conductance, drain, in_sem,
+    prior, material, probe, misfit, conductance, drain, in_sem,
     w, cond, keep, loss, rate, old, red,
     seen, mate_vent, my_vent, mate_red, gain, base, high_red, high_rate,
     chain_in, chain_out, swap_out, swap_in, carried,
@@ -43,7 +43,7 @@
     chunks = half * CUT
     part = across // 2 // CUT
     inner = pl.ds(1, planes - 2)
-    small = [(probe_in, probe), (misfit_in, misfit), (vent_in, vent), (conductance_in, conductance), (drain_in, drain)]
+    small = [(probe_in, probe), (misfit_in, misfit), (conductance_in, conductance), (drain_in, drain)]
     faces, body = [], []
     for i in (0, planes - 1):
         faces += [(prior_in.at[0, i], prior.at[0, i]), (material_in.at[i], material.at[i])]
@@ -324,13 +324,13 @@
     return pl.pallas_call(
         functools.partial(kernel, slabs, tiles),
         out_shape=jax.ShapeDtypeStruct(prior.shape, F32),
-        in_specs=[hbm] * 7,
+        in_specs=[hbm] * 6 + [pl.BlockSpec(memory_space=pltpu.SMEM)],
         out_specs=vmem,
         scratch_shapes=[
             pltpu.VMEM(prior.shape, F32), pltpu.VMEM(material.shape, jnp.int32),
             pltpu.VMEM((1, sensors), jnp.int32), pltpu.VMEM(misfit.shape, F32),
-            pltpu.SMEM(vent.shape, F32), pltpu.SMEM(conductance.shape, F32), pltpu.SMEM(drain.shape, F32),
-            dma((11,)),
+            pltpu.SMEM(conductance.shape, F32), pltpu.SMEM(drain.shape, F32),
+            dma((10,)),
             pltpu.VMEM((FINE_STEPS, planes + 2, across + 2 * PAD, depth), F32),
             whole, whole, whole, quarter, quarter, quarter,
             pltpu.VMEM((3, depth, sensors), BF16),
@@ -340,9 +340,12 @@
             dma((chunks,)), dma((chunks,)), dma((chunks,)), dma((chunks,)), dma((chunks,)), dma((chunks,)),
         ],
         compiler_params=pltpu.CompilerParams(
-            collective_id=0, has_side_effects=True, vmem_limit_bytes=60 * 1024 * 1024
+            collective_id=0, has_side_effects=True, vmem_limit_bytes=48 * 1024 * 1024
         ),
-    )(prior, material, probe.reshape(1, sensors), misfit, vent, conductance, drain)
+    )(*[
+        pltpu.with_memory_space_constraint(array, pltpu.HBM)
+        for array in (prior, material, probe.reshape(1, sensors), misfit, conductance, drain)
+    ], vent)
 
 
 def solution(mesh):

time: 34.4 us -> 32.1 us (0.933)
  local copies, waits for them, and re-layouts: 2.3 us -> 0.97 us
  Pallas kernels: 31.3 us -> 30.3 us
    unnamed x1, local copies, waits for them, and re-layouts: 2.3 us -> 0.97 us
    pallas_call x1, Pallas kernels: 31.3 us -> 30.3 us  [on_device(): pl.pallas_call(functools.partial(kernel, slabs, tiles), out_shape=jax.Sha...]
where the time goes in v3:
time: 32.1 us; the launch traced here: 31.9 us
  Pallas kernels  30.3 us (94%)
  local copies, waits for them, and re-layouts  0.97 us (3%)
  between operations  0.66 us (2%)
    pallas_call x1, Pallas kernels, on_device(): pl.pallas_call(functools.partial(kernel, slabs, tiles), out_shape=jax.Sha...  30.3 us
    unnamed x1, local copies, waits for them, and re-layouts  0.97 us

profile of v3, /device:TPU:0, one launch (start us, length us, event | category | flops | bytes accessed | tf_op | source)
XLA Modules:
  0.0 31.9 jit_solution(3419691101384926545)
XLA Ops:
  0.7 30.3 %shard_map.73 = f32[1,16,128,128]{3,2,1,0:T(8,128)S(1)} custom-call(f32[1,16,128,128]{3,2,1,0:T(8,128)} %prior_in.1, s32[16,128,128]{2,1,0:T(8,128)} %material_in.1, s32[1,64]{1,0:T(1,128)} %bitcast.1, f32[1,64]{1,0:T(1,128)} %misfit_in.1, f32[8]{0:T(128)} %conductance_in.1, f32[8]{0:T(128)} %drain_in.1, f32[1]{0:T(128)S(6)} %copy.9.vent), custom_call_target="tpu_custom_call" | custom-call | tf_op jit(solution)/shard_map/pallas_call | solution.py:324
  31.0 1.0 %copy.10 = f32[1,16,128,128]{3,2,1,0:T(8,128)} copy(f32[1,16,128,128]{3,2,1,0:T(8,128)S(1)} %shard_map.73) | data formatting | bytes 2097152
